TPU v7x, 512 devices: a whole 4x4x16 slice. The times are simulated.
512 devices in a mesh: pipe: 4 (over z_hi), dp: 16 (over y, x), tensor: 8 (over z_lo, core).
Axes of the slice: x: 4, y: 4, z: 16 (z_hi: 4, z_lo: 4; z = z_hi * 4 + z_lo), core: 2. Of those that a mesh axis runs over, the one named last changes fastest.
Arguments:
- x_in: bfloat16 [4, 2, 16, 128, 1600], P('pipe', None, 'dp', 'tensor'), may hold values from -6 to 6
- out_grad: bfloat16 [2, 16, 128, 1600], P(None, 'dp'), may hold values from -6 to 6
- layer_scale: float32 [4, 1600], P('pipe'), may hold values from 0.05 to 1
- norm_gain: float32 [4, 1600], P('pipe'), may hold values from 0.5 to 1.5
- master: float32 [4, 1600, 8192], P('pipe', 'dp', 'tensor'), may hold values from -0.15625 to 0.15625
- moment_one: float32 [4, 1600, 8192], P('pipe', 'dp', 'tensor'), may hold values from -4 to 4
- moment_two: float32 [4, 1600, 8192], P('pipe', 'dp', 'tensor'), may hold values from 0.05 to 5
Outputs:
- input_grads: bfloat16 [4, 2, 16, 128, 1600], P('pipe', None, 'dp', 'tensor')
- new_master: float32 [4, 1600, 8192], P('pipe', 'dp', 'tensor')
- new_moment_one: float32 [4, 1600, 8192], P('pipe', 'dp', 'tensor')
- new_moment_two: float32 [4, 1600, 8192], P('pipe', 'dp', 'tensor')
- scale_grads: float32 [4, 2, 1600], P('pipe')
All inputs are finite; a program needn't handle non-finite values.
Results may differ from a plain program's by a relative error of at most 0.027.
Values may be sent and summed in bfloat16 or wider, within the bound.
A program may use at most 128 MiB of HBM per device.

v0:
```python
import math
import jax
import jax.numpy as jnp
from jax import lax
from jax.sharding import PartitionSpec as P

HD = 128
beta_one = 0.9
beta_two = 0.95
adam_eps = 1e-08
learn_rate = 0.001
weight_decay = 0.05
adam_step = 100.0
norm_eps = 1e-06


def from_behind(block, axis, distance):
    devices = range(lax.axis_size(axis))
    route = [(i - distance, i) for i in devices if i - distance in devices]
    return lax.ppermute(block, axis, route)


def normalize(values_in):
    inverse = lax.rsqrt(jnp.mean(values_in * values_in, axis=-1, keepdims=True) + norm_eps)
    return (inverse, values_in * inverse)


def select_micro(array, micro_index):
    return lax.dynamic_index_in_dim(array, micro_index, 0, keepdims=False)


def store_slot(buffer, value, slot_index):
    return lax.dynamic_update_index_in_dim(buffer, value, slot_index, 0)


def local(x_in, out_grad, layer_scale, norm_gain, master, moment_one, moment_two):
    n_pipe = lax.axis_size("pipe")
    n_tensor = lax.axis_size("tensor")
    pipe_rank = lax.axis_index("pipe")
    micro_count = x_in.shape[1]
    images = x_in.shape[2]
    shard_len = x_in.shape[3]
    channels = x_in.shape[4]
    seq_len = shard_len * n_tensor
    row_start = lax.axis_index("tensor") * shard_len
    head_cols = master.shape[2] // 4
    local_heads = head_cols // HD
    score_root = math.sqrt(HD)
    scale_vec = layer_scale[0]
    gain_vec = norm_gain[0]
    weights = lax.all_gather(master[0].astype(jnp.bfloat16), "dp", axis=0, tiled=True)
    w_qkv = weights[:, : 3 * head_cols]
    w_out = weights[:, 3 * head_cols :]
    full_x = lax.all_gather(x_in[0], "tensor", axis=2, tiled=True).astype(jnp.float32)
    full_inverse, full_unit = normalize(full_x)
    normed = (full_unit * gain_vec).astype(jnp.bfloat16)
    local_unit = lax.dynamic_slice_in_dim(full_unit, row_start, shard_len, 2)
    projected = jnp.einsum(
        "mbsd,dc->mbsc", normed, w_qkv, preferred_element_type=jnp.float32
    ).astype(jnp.bfloat16)
    projected = projected.reshape(micro_count, images, seq_len, 3, local_heads, HD)
    query = projected[:, :, :, 0]
    keys = projected[:, :, :, 1]
    values = projected[:, :, :, 2]
    scores = (
        jnp.einsum("mbqhe,mbkhe->mbhqk", query, keys, preferred_element_type=jnp.float32)
        / score_root
    )
    probs = jax.nn.softmax(scores, axis=-1)
    probs_low = probs.astype(jnp.bfloat16)
    attended = jnp.einsum(
        "mbhqk,mbkhe->mbqhe", probs_low, values, preferred_element_type=jnp.float32
    ).astype(jnp.bfloat16)
    attended_flat = attended.reshape(micro_count, images, seq_len, head_cols)

    def backward_segment(micro_index, incoming):
        query_now = select_micro(query, micro_index)
        keys_now = select_micro(keys, micro_index)
        values_now = select_micro(values, micro_index)
        probs_now = select_micro(probs, micro_index)
        probs_low_now = select_micro(probs_low, micro_index)
        attended_now = select_micro(attended, micro_index)
        scaled = (scale_vec * incoming.astype(jnp.float32)).astype(jnp.bfloat16)
        d_att = jnp.einsum("bsd,dc->bsc", scaled, w_out, preferred_element_type=jnp.float32).astype(
            jnp.bfloat16
        )
        d_att = d_att.reshape(images, seq_len, local_heads, HD)
        d_prob = jnp.einsum(
            "bqhe,bkhe->bhqk", d_att, values_now, preferred_element_type=jnp.float32
        )
        row_delta = jnp.einsum(
            "bqhe,bqhe->bhq", d_att, attended_now, preferred_element_type=jnp.float32
        )
        d_score = (probs_now * (d_prob - row_delta[..., None]) / score_root).astype(jnp.bfloat16)
        d_query = jnp.einsum(
            "bhqk,bkhe->bqhe", d_score, keys_now, preferred_element_type=jnp.float32
        ).astype(jnp.bfloat16)
        d_keys = jnp.einsum(
            "bhqk,bqhe->bkhe", d_score, query_now, preferred_element_type=jnp.float32
        ).astype(jnp.bfloat16)
        d_values = jnp.einsum(
            "bhqk,bqhe->bkhe", probs_low_now, d_att, preferred_element_type=jnp.float32
        ).astype(jnp.bfloat16)
        d_proj = jnp.concatenate([d_query, d_keys, d_values], axis=2).reshape(
            images, seq_len, 3 * head_cols
        )
        partial_sum = jnp.einsum("bsc,dc->bsd", d_proj, w_qkv, preferred_element_type=jnp.float32)
        return (partial_sum, d_proj, scaled)

    def spare_segment(micro_index, incoming):
        return (
            jnp.zeros((images, seq_len, channels), jnp.float32),
            jnp.zeros((images, seq_len, 3 * head_cols), jnp.bfloat16),
            jnp.zeros((images, seq_len, channels), jnp.bfloat16),
        )

    segments = n_pipe + micro_count - 1
    is_last = pipe_rank == n_pipe - 1
    received = jnp.zeros((images, seq_len, channels), jnp.bfloat16)
    slots = micro_count + 1
    grads_out = jnp.zeros((slots, images, shard_len, channels), jnp.bfloat16)
    proj_saved = jnp.zeros((slots, images, seq_len, 3 * head_cols), jnp.bfloat16)
    scaled_saved = jnp.zeros((slots, images, seq_len, channels), jnp.bfloat16)
    grad_saved = jnp.zeros((slots, images, seq_len, channels), jnp.bfloat16)
    gain_part = jnp.zeros((channels,), jnp.float32)
    for segment_step in range(segments):
        micro_index = segment_step - (n_pipe - 1) + pipe_rank
        active = jnp.logical_and(micro_index >= 0, micro_index < micro_count)
        micro_index = jnp.clip(micro_index, 0, micro_count - 1)
        slot_index = jnp.where(active, micro_index, micro_count)
        arrived = received
        incoming = jnp.where(is_last, select_micro(out_grad, micro_index), arrived)
        partial_sum, d_proj, scaled = lax.cond(
            active, backward_segment, spare_segment, micro_index, incoming
        )
        pieces = partial_sum.astype(jnp.bfloat16).reshape(images, n_tensor, shard_len, channels)
        landed = lax.all_to_all(pieces, "tensor", split_axis=1, concat_axis=1, tiled=True)
        own_d = jnp.sum(landed.astype(jnp.float32), axis=1)
        d_normed = lax.all_gather(own_d.astype(jnp.bfloat16), "tensor", axis=1, tiled=True).astype(
            own_d.dtype
        )
        own_unit = select_micro(local_unit, micro_index)
        sel_unit = select_micro(full_unit, micro_index)
        sel_inverse = select_micro(full_inverse, micro_index)
        d_unit = d_normed * gain_vec
        d_input = sel_inverse * (
            d_unit - sel_unit * jnp.mean(d_unit * sel_unit, axis=-1, keepdims=True)
        )
        passed = (incoming.astype(jnp.float32) + d_input).astype(jnp.bfloat16)
        own_passed = lax.dynamic_slice_in_dim(passed, row_start, shard_len, 1)
        gain_part = gain_part + jnp.where(active, jnp.sum(own_d * own_unit, axis=(0, 1)), 0.0)
        grads_out = store_slot(grads_out, own_passed, slot_index)
        proj_saved = store_slot(proj_saved, d_proj, slot_index)
        scaled_saved = store_slot(scaled_saved, scaled, slot_index)
        grad_saved = store_slot(grad_saved, incoming, slot_index)
        if segment_step + 1 < segments:
            received = from_behind(passed, "pipe", -1)
    grads_kept = grads_out[:micro_count]
    proj_kept = proj_saved[:micro_count]
    scaled_kept = scaled_saved[:micro_count]
    grad_kept = grad_saved[:micro_count]
    grad_qkv = jnp.einsum("mbsd,mbsc->dc", normed, proj_kept, preferred_element_type=jnp.float32)
    grad_out = jnp.einsum(
        "mbsd,mbsc->dc", scaled_kept, attended_flat, preferred_element_type=jnp.float32
    )
    weight_grad = lax.psum_scatter(
        jnp.concatenate([grad_qkv, grad_out], axis=1).astype(jnp.bfloat16),
        "dp",
        scatter_dimension=0,
        tiled=True,
    ).astype(jnp.float32)
    summed_out = jnp.einsum(
        "mbsd,mbsc->dc", grad_kept, attended_flat, preferred_element_type=jnp.float32
    )
    scale_part = jnp.sum(w_out.astype(jnp.float32) * summed_out, axis=1)
    scale_grad, gain_grad = lax.psum((scale_part, gain_part), ("dp", "tensor"))
    bias_one = 1.0 - beta_one**adam_step
    bias_two = 1.0 - beta_two**adam_step
    first_new = beta_one * moment_one[0] + (1.0 - beta_one) * weight_grad
    second_new = beta_two * moment_two[0] + (1.0 - beta_two) * weight_grad * weight_grad
    update = first_new / bias_one / (jnp.sqrt(second_new / bias_two) + adam_eps)
    master_new = master[0] - learn_rate * (update + weight_decay * master[0])
    scale_both = jnp.stack([scale_grad, gain_grad])
    return (grads_kept[None], master_new[None], first_new[None], second_new[None], scale_both[None])


def solution(mesh):
    placed = (
        P("pipe", None, "dp", "tensor", None),
        P(None, "dp", None, None),
        P("pipe", None),
        P("pipe", None),
        P("pipe", "dp", "tensor"),
        P("pipe", "dp", "tensor"),
        P("pipe", "dp", "tensor"),
    )
    return jax.shard_map(
        local,
        mesh=mesh,
        in_specs=placed,
        out_specs=(
            P("pipe", None, "dp", "tensor", None),
            P("pipe", "dp", "tensor"),
            P("pipe", "dp", "tensor"),
            P("pipe", "dp", "tensor"),
            P("pipe", None, None),
        ),
        check_vma=False,
    )
```

profile of v0, /device:TPU:128, one launch (start us, length us, event | category | flops | bytes accessed | tf_op | source)
XLA Modules:
  0.0 1397.1 jit_solution(9497189529222593364)
XLA Ops:
  9.8 17.2 %all-gather = bf16[1,2,1,128,1600]{4,3,2,1,0:T(8,128)(2,1)S(1)} all-gather(bf16[1,2,1,16,1600]{4,3,2,1,0:T(8,128)(2,1)} %param.17), channel_id=2, replica_groups=mesh['pipe'=4,'dp'=16,'tensor'=8] {'tensor'}, dimensions={3}, use_global_device_ids=true | all-gather | bytes 921600 | tf_op jit(solution)/shard_map/all_gather | solution.py:54
  28.1 50.7 %all-gather.9.cloned.1.call-done = bf16[16,100,1024]{2,1,0:T(8,128)(2,1)} async-done(((bf16[1,100,1024]{2,1,0:T(8,128)(2,1)}), bf16[16,100,1024]{2,1,0:T(8,128)(2,1)}) %all-gather.9.cloned.1.call-update) | async-done | bytes 3276816 | tf_op jit(solution)/shard_map/all_gather | solution.py:51
  78.8 2.9 reshape.819
  81.7 3.4 fusion.113
  96.1 2.1 convolution_convert_fusion.20
  98.2 2.3 conditional.5
  100.5 2.0 copy.213
  102.5 4.8 all-to-all-start
  108.7 2.3 constant_dynamic-slice_fusion
  111.4 2.4 copy.217
  115.1 5.5 all-to-all-done
  122.4 15.6 %all-gather.1 = bf16[128,1600]{1,0:T(8,128)(2,1)} all-gather(bf16[16,1600]{1,0:T(8,128)(2,1)S(1)} %convert_element_type.421), channel_id=3, replica_groups=mesh['pipe'=4,'dp'=16,'tensor'=8] {'tensor'}, dimensions={0}, use_global_device_ids=true | all-gather | bytes 460800 | tf_op jit(solution)/shard_map/all_gather | solution.py:139
  138.0 1.9 copy.216
  141.5 2.2 fusion.145
  143.8 2.1 collective-permute-start
  147.2 39.6 %collective-permute-done = bf16[1,128,1600]{1,2,0:T(8,128)(2,1)} collective-permute-done((bf16[1,128,1600]{1,2,0:T(8,128)(2,1)}, bf16[1,128,1600]{1,2,0:T(8,128)(2,1)}, u32[]{:S(2)}, u32[]{:S(2)}) %collective-permute-start) | collective-permute-done | bytes 409632 | tf_op jit(solution)/shard_map/ppermute | solution.py:20
  186.9 1.9 bitcast_dynamic-update-slice_fusion.2
  189.9 2.7 conditional.6
  192.6 2.0 copy.227
  194.6 4.1 all-to-all-start.1
  198.7 2.4 copy.231
  201.1 10.9 all-to-all-done.1
  213.7 15.6 %all-gather.2 = bf16[128,1600]{1,0:T(8,128)(2,1)} all-gather(bf16[16,1600]{1,0:T(8,128)(2,1)S(1)} %convert_element_type.429), channel_id=4, replica_groups=mesh['pipe'=4,'dp'=16,'tensor'=8] {'tensor'}, dimensions={0}, use_global_device_ids=true | all-gather | bytes 460800 | tf_op jit(solution)/shard_map/all_gather | solution.py:139
  229.2 2.0 copy.230
  232.9 2.2 fusion.139
  235.1 2.2 collective-permute-start.1
  237.3 98.2 %collective-permute-done.1 = bf16[1,128,1600]{1,2,0:T(8,128)(2,1)} collective-permute-done((bf16[1,128,1600]{1,2,0:T(8,128)(2,1)}, bf16[1,128,1600]{1,2,0:T(8,128)(2,1)}, u32[]{:S(2)}, u32[]{:S(2)}) %collective-permute-start.1) | collective-permute-done | bytes 409632 | tf_op jit(solution)/shard_map/ppermute | solution.py:20
  335.5 2.1 bitcast_dynamic-update-slice_fusion.1
  337.7 34.1 %conditional.7 = (bf16[1,128,1600]{1,2,0:T(8,128)(2,1)}, bf16[1,1,128,768]{3,2,0,1:T(8,128)(2,1)}, bf16[1,1,128,1600]{2,3,0,1:T(8,128)(2,1)}) conditional(s32[]{:T(128)} %convert_element_type.434, () %tuple.72, (s32[]{:T(128)}, bf16[2,1,128,2,128]{4,2,3,0,1:T(8,128)(2,1)}, f32[2,1,2,128,128]{3,4,2,0,1:T(8,128)S(1)}, f32[1,1600]{1,0:T(1,128)S(1)}, ...), branch_computations={%region_11.12_spmd, %region_12.13_spmd} | conditional | flops 454803200 | bytes 11565162 | solution.py:133
  337.7 2.0 copy.236
  340.3 1.9 convolution_convert_fusion.8
  369.8 2.0 copy.364
  371.8 2.0 copy.241
  373.8 4.1 all-to-all-start.2
  377.9 2.3 copy.245
  380.3 2.3 copy.259
  382.6 2.4 copy.273
  399.1 16.0 %all-gather.3 = bf16[128,1600]{1,0:T(8,128)(2,1)} all-gather(bf16[16,1600]{1,0:T(8,128)(2,1)S(1)} %convert_element_type.437), channel_id=5, replica_groups=mesh['pipe'=4,'dp'=16,'tensor'=8] {'tensor'}, dimensions={0}, use_global_device_ids=true | all-gather | bytes 460800 | tf_op jit(solution)/shard_map/all_gather | solution.py:139
  415.0 1.9 copy.244
  425.6 38.5 %collective-permute-done.2 = bf16[1,128,1600]{1,2,0:T(8,128)(2,1)S(1)} collective-permute-done((bf16[1,128,1600]{1,2,0:T(8,128)(2,1)S(1)}, bf16[1,128,1600]{1,2,0:T(8,128)(2,1)S(1)}, u32[]{:S(2)}, u32[]{:S(2)}) %collective-permute-start.2) | collective-permute-done | bytes 409632 | tf_op jit(solution)/shard_map/ppermute | solution.py:20
  465.1 34.2 %conditional.8 = (bf16[1,128,1600]{1,2,0:T(8,128)(2,1)}, bf16[1,1,128,768]{3,2,0,1:T(8,128)(2,1)}, bf16[1,1,128,1600]{2,3,0,1:T(8,128)(2,1)}) conditional(s32[]{:T(128)} %convert_element_type.442, () %tuple.74, (s32[]{:T(128)}, bf16[2,1,128,2,128]{4,2,3,0,1:T(8,128)(2,1)}, f32[2,1,2,128,128]{3,4,2,0,1:T(8,128)S(1)}, f32[1,1600]{1,0:T(1,128)S(1)}, ...), branch_computations={%region_15.16_spmd, %region_16.17_spmd} | conditional | flops 454803200 | bytes 11565162 | solution.py:133
  465.2 2.0 copy.250
  467.8 1.9 convolution_convert_fusion.12
  497.4 1.9 copy.368
  499.3 2.0 copy.255
  501.3 4.1 all-to-all-start.3
  505.4 1.9 dynamic-slice_bitcast_fusion.2
  524.3 16.0 %all-gather.4 = bf16[128,1600]{1,0:T(8,128)(2,1)} all-gather(bf16[16,1600]{1,0:T(8,128)(2,1)S(1)} %convert_element_type.445), channel_id=6, replica_groups=mesh['pipe'=4,'dp'=16,'tensor'=8] {'tensor'}, dimensions={0}, use_global_device_ids=true | all-gather | bytes 460800 | tf_op jit(solution)/shard_map/all_gather | solution.py:139
  540.3 1.9 copy.258
  543.9 2.2 fusion.127
  546.1 2.1 collective-permute-start.3
  548.2 1.9 dynamic-slice_bitcast_fusion
  553.3 36.9 %collective-permute-done.3 = bf16[1,128,1600]{1,2,0:T(8,128)(2,1)} collective-permute-done((bf16[1,128,1600]{1,2,0:T(8,128)(2,1)}, bf16[1,128,1600]{1,2,0:T(8,128)(2,1)}, u32[]{:S(2)}, u32[]{:S(2)}) %collective-permute-start.3) | collective-permute-done | bytes 409632 | tf_op jit(solution)/shard_map/ppermute | solution.py:20
  590.2 2.2 bitcast_dynamic-update-slice_fusion.3
  592.4 2.3 conditional.9
  594.7 2.0 copy.269
  596.7 4.1 all-to-all-start.4
  602.5 1.9 bitcast_convert_fusion
  608.2 76.2 %fusion = bf16[112,1024]{1,0:T(8,128)(2,1)} fusion(bf16[1600,1024]{1,0:T(8,128)(2,1)S(1)} %pad_maximum_fusion.5), kind=kCustom, calls=%all-reduce-scatter | all-reduce-scatter fusion | flops 1835009 | bytes 3508224
  685.4 3.7 collective-permute-start.4
  689.1 4.1 collective-permute-start.5
  693.2 2.0 fusion.112
  703.2 15.6 %all-gather.5 = bf16[128,1600]{1,0:T(8,128)(2,1)S(1)} all-gather(bf16[16,1600]{1,0:T(8,128)(2,1)S(1)} %get-tuple-element.430), channel_id=7, replica_groups=mesh['pipe'=4,'dp'=16,'tensor'=8] {'tensor'}, dimensions={0}, use_global_device_ids=true | all-gather | bytes 460800 | tf_op jit(solution)/shard_map/all_gather | solution.py:139
  721.0 668.4 %all-reduce.2 = (f32[1,1600]{1,0:T(1,128)S(1)}, f32[1,1600]{1,0:T(1,128)S(1)}) all-reduce(f32[1,1600]{1,0:T(1,128)S(1)} %stack.10, f32[1,1600]{1,0:T(1,128)S(1)} %stack.9), channel_id=1, replica_groups=mesh['pipe'=4,'dp'=16,'tensor'=8] {'dp','tensor'}, use_global_device_ids=true, to_apply=%region_31.32 | all-reduce | flops 3200 | bytes 25600 | tf_op jit(solution)/shard_map/psum | solution.py:176
  (215 shorter events, 151.9 us)
Async XLA Ops:
  7.2 20.1 %copy-start.2 = (bf16[2,1,128,1600]{2,3,1,0:T(8,128)(2,1)S(1)}, bf16[2,1,128,1600]{2,3,1,0:T(8,128)(2,1)}, u32[]{:S(2)}) copy-start(bf16[2,1,128,1600]{2,3,1,0:T(8,128)(2,1)} %param.18) | copy-start | bytes 2457604
  7.2 71.6 %all-gather.9.cloned.1.call-start = ((), (), s32[]{:S(2)}) async-start(), calls=%async_computation.5 | async-start | bytes 3620864 | tf_op jit(solution)/shard_map/all_gather | solution.py:51
  27.0 1.1 copy-start.5
  27.3 54.4 %copy-start.44 = (f32[2,128]{1,0:T(2,128)}, f32[2,128]{1,0:T(2,128)S(1)}, u32[]{:S(2)}) copy-start(f32[2,128]{1,0:T(2,128)S(1)} %add_rsqrt_fusion) | copy-start | bytes 3076
  81.7 3.5 copy-start.1
  88.3 0.8 copy-start.35
  88.3 5.4 copy-start.34
  93.7 4.5 copy-start.42
  102.5 18.2 %all-to-all-start = ((bf16[1,8,16,1600]{3,2,0,1:T(8,128)(2,1)}), bf16[1,8,16,1600]{3,2,0,1:T(8,128)(2,1)}, u32[]{:S(2)}, u32[]{:S(2)}) async-start(bf16[1,8,16,1600]{3,2,0,1:T(8,128)(2,1)} %bitcast.535), calls=%async_computation | async-start | bytes 851968 | tf_op jit(solution)/shard_map/all_to_all | solution.py:137
  108.6 2.7 copy-start
  121.7 0.6 copy-start.26
  139.9 1.6 copy-start.11
  143.8 43.1 %collective-permute-start = (bf16[1,128,1600]{1,2,0:T(8,128)(2,1)}, bf16[1,128,1600]{1,2,0:T(8,128)(2,1)}, u32[]{:S(2)}, u32[]{:S(2)}) collective-permute-start(bf16[1,128,1600]{1,2,0:T(8,128)(2,1)} %fusion.145), channel_id=1, source_target_pairs={{128,0},{256,128},{384,256},{129,1},{257,129},{385,257},{130,2},{2... | collective-permute-start | bytes 1228808 | tf_op jit(solution)/shard_map/ppermute | solution.py:20
  145.9 41.0 %copy-start.3 = (bf16[2,1,128,1600]{2,3,1,0:T(8,128)(2,1)S(1)}, bf16[2,1,128,1600]{2,3,1,0:T(8,128)(2,1)}, u32[]{:S(2)}) copy-start(bf16[2,1,128,1600]{2,3,1,0:T(8,128)(2,1)} %param.18) | copy-start | bytes 2457604
  188.8 1.1 copy-start.25
  194.6 17.4 %all-to-all-start.1 = ((bf16[1,8,16,1600]{3,2,0,1:T(8,128)(2,1)}), bf16[1,8,16,1600]{3,2,0,1:T(8,128)(2,1)}, u32[]{:S(2)}, u32[]{:S(2)}) async-start(bf16[1,8,16,1600]{3,2,0,1:T(8,128)(2,1)} %bitcast.537), calls=%async_computation.1 | async-start | bytes 851968 | tf_op jit(solution)/shard_map/all_to_all | solution.py:137
  213.0 0.6 copy-start.28
  231.2 1.6 copy-start.9
  235.1 100.4 %collective-permute-start.1 = (bf16[1,128,1600]{1,2,0:T(8,128)(2,1)}, bf16[1,128,1600]{1,2,0:T(8,128)(2,1)}, u32[]{:S(2)}, u32[]{:S(2)}) collective-permute-start(bf16[1,128,1600]{1,2,0:T(8,128)(2,1)} %fusion.139), channel_id=1, source_target_pairs={{128,0},{256,128},{384,256},{129,1},{257,129},{385,257},{130,2},{2... | collective-permute-start | bytes 1228808 | tf_op jit(solution)/shard_map/ppermute | solution.py:20
  364.7 1.6 copy-start.20
  373.8 23.6 %all-to-all-start.2 = ((bf16[1,8,16,1600]{3,2,0,1:T(8,128)(2,1)}), bf16[1,8,16,1600]{3,2,0,1:T(8,128)(2,1)}, u32[]{:S(2)}, u32[]{:S(2)}) async-start(bf16[1,8,16,1600]{3,2,0,1:T(8,128)(2,1)} %bitcast.534), calls=%async_computation.2 | async-start | bytes 851968 | tf_op jit(solution)/shard_map/all_to_all | solution.py:137
  398.4 0.7 copy-start.30
  417.0 1.6 copy-start.8
  417.0 5.1 copy-start.41
  418.6 45.4 %copy-start.4 = (bf16[2,1,128,1600]{2,3,1,0:T(8,128)(2,1)S(1)}, bf16[2,1,128,1600]{2,3,1,0:T(8,128)(2,1)}, u32[]{:S(2)}) copy-start(bf16[2,1,128,1600]{2,3,1,0:T(8,128)(2,1)} %param.18) | copy-start | bytes 2457604
  420.1 45.0 %copy-start.22 = (bf16[1,128,1600]{1,2,0:T(8,128)(2,1)}, bf16[1,128,1600]{1,2,0:T(8,128)(2,1)S(1)}, u32[]{:S(2)}) copy-start(bf16[1,128,1600]{1,2,0:T(8,128)(2,1)S(1)} %fusion.133) | copy-start | bytes 1228804
  420.1 43.9 %collective-permute-start.2 = (bf16[1,128,1600]{1,2,0:T(8,128)(2,1)S(1)}, bf16[1,128,1600]{1,2,0:T(8,128)(2,1)S(1)}, u32[]{:S(2)}, u32[]{:S(2)}) collective-permute-start(bf16[1,128,1600]{1,2,0:T(8,128)(2,1)S(1)} %fusion.133), channel_id=1, source_target_pairs={{128,0},{256,128},{384,256},{129,1},{257,129},{385,257},{130,2},{2... | collective-permute-start | bytes 1228808 | tf_op jit(solution)/shard_map/ppermute | solution.py:20
  422.1 43.0 %copy-start.36 = (bf16[3,1,16,1600]{3,2,0,1:T(8,128)(2,1)}, bf16[3,1,16,1600]{3,2,0,1:T(8,128)(2,1)S(1)}, u32[]{:S(2)}) copy-start(bf16[3,1,16,1600]{3,2,0,1:T(8,128)(2,1)S(1)} %constant_dynamic-update-slice_fusion.14) | copy-start | bytes 460804
  492.2 1.6 copy-start.21
  501.3 21.3 %all-to-all-start.3 = ((bf16[1,8,16,1600]{3,2,0,1:T(8,128)(2,1)}), bf16[1,8,16,1600]{3,2,0,1:T(8,128)(2,1)}, u32[]{:S(2)}, u32[]{:S(2)}) async-start(bf16[1,8,16,1600]{3,2,0,1:T(8,128)(2,1)} %bitcast.536), calls=%async_computation.3 | async-start | bytes 851968 | tf_op jit(solution)/shard_map/all_to_all | solution.py:137
  523.7 0.6 copy-start.32
  542.3 1.6 copy-start.7
  546.1 44.2 %collective-permute-start.3 = (bf16[1,128,1600]{1,2,0:T(8,128)(2,1)}, bf16[1,128,1600]{1,2,0:T(8,128)(2,1)}, u32[]{:S(2)}, u32[]{:S(2)}) collective-permute-start(bf16[1,128,1600]{1,2,0:T(8,128)(2,1)} %fusion.127), channel_id=1, source_target_pairs={{128,0},{256,128},{384,256},{129,1},{257,129},{385,257},{130,2},{2... | collective-permute-start | bytes 1228808 | tf_op jit(solution)/shard_map/ppermute | solution.py:20
  594.7 7.8 copy-start.6
  594.7 7.8 copy-start.45
  596.7 103.9 %all-to-all-start.4 = ((bf16[1,8,16,1600]{3,2,0,1:T(8,128)(2,1)}), bf16[1,8,16,1600]{3,2,0,1:T(8,128)(2,1)}, u32[]{:S(2)}, u32[]{:S(2)}) async-start(bf16[1,8,16,1600]{3,2,0,1:T(8,128)(2,1)} %bitcast.151), calls=%async_computation.4 | async-start | bytes 851968 | tf_op jit(solution)/shard_map/all_to_all | solution.py:137
  602.5 3.8 copy-start.12
  684.4 11.5 copy-start.24
  685.4 10.5 collective-permute-start.4
  689.1 6.8 collective-permute-start.5
  693.2 3.4 copy-start.23
  693.2 3.4 copy-start.38
  693.2 3.4 copy-start.39
  697.1 4.7 copy-start.27
  697.1 4.7 copy-start.29
  697.1 4.7 copy-start.31
  697.1 4.7 copy-start.33
  700.6 18.5 %copy-start.10 = (f32[1,1,128,1600]{2,3,1,0:T(8,128)S(1)}, f32[1,1,128,1600]{2,3,1,0:T(8,128)}, u32[]{:S(2)}) copy-start(f32[1,1,128,1600]{2,3,1,0:T(8,128)} %copy.273) | copy-start | bytes 2457604
  703.2 16.3 %copy-start.17 = (bf16[1,128,1600]{1,2,0:T(8,128)(2,1)S(1)}, bf16[1,128,1600]{1,2,0:T(8,128)(2,1)}, u32[]{:S(2)}) copy-start(bf16[1,128,1600]{1,2,0:T(8,128)(2,1)} %get-tuple-element.408) | copy-start | bytes 1228804
  703.2 16.3 %copy-start.46 = (f32[16]{0:T(128)S(1)}, f32[16]{0:T(128)}, u32[]{:S(2)}) copy-start(f32[16]{0:T(128)} %dynamic-slice.8) | copy-start | bytes 196
  719.4 0.9 copy-start.37
Sparse Core Ops, SparseCore 0:
  11.6 67.1 all-gather.8
where the time goes:
time: 1410 us; the launch traced here: 1400 us
  blocking collectives  840 us (60%)
  waiting for transfers between devices  281 us (20%)
  local copies, waits for them, and re-layouts  143 us (10%)
  other arithmetic  47.2 us (3%)
  starting transfers between devices  37.3 us (3%)
  matrix products  31.9 us (2%)
  between operations  15.6 us (1%)
    psum x1, blocking collectives, local(): scale_grad, gain_grad = lax.psum((scale_part, gain_part), ('dp', 'tensor'))  668 us
    ppermute x4, waiting for transfers between devices, from_behind(): return lax.ppermute(block, axis, route)  213 us
    all_gather x5, blocking collectives, local(): lax.all_gather(own_d.astype(jnp.bfloat16), 'tensor', axis=1, tiled=True)  78.7 us
    unnamed x1, blocking collectives  76.2 us
    all_gather x1, waiting for transfers between devices, local(): lax.all_gather(master[0].astype(jnp.bfloat16), 'dp', axis=0, tiled=True)  50.7 us
    another operation x23, local copies, waits for them, and re-layouts  32.1 us
  transfers between devices with their start and end apart: 12, of which 8 were waited for; matrix products, arithmetic and copies ran while one was open for 11% of the time, Pallas kernels for 0%

commit v1 on v0

--- a/solution.py
+++ b/solution.py
@@ -173,7 +173,9 @@
         "mbsd,mbsc->dc", grad_kept, attended_flat, preferred_element_type=jnp.float32
     )
     scale_part = jnp.sum(w_out.astype(jnp.float32) * summed_out, axis=1)
-    scale_grad, gain_grad = lax.psum((scale_part, gain_part), ("dp", "tensor"))
+    scale_grad, gain_grad = jax.lax.psum(
+        jax.lax.psum((scale_part, gain_part), axis_name="dp"), axis_name="tensor"
+    )
     bias_one = 1.0 - beta_one**adam_step
     bias_two = 1.0 - beta_two**adam_step
     first_new = beta_one * moment_one[0] + (1.0 - beta_one) * weight_grad

time: 1410 us -> 838 us (0.59)
  blocking collectives: 840 us -> 270 us
    psum x1 -> x2, blocking collectives: 668 us -> 97.7 us  [the longest x1 71.7 us: local(): jax.lax.psum((scale_part, gain_part), axis_name='dp')]
  transfers between devices with their start and end apart: 12 -> 12, of which waited for: 8 -> 8; matrix products, arithmetic and copies ran while one was open for 11% -> 18% of each run, Pallas kernels for 0% -> 0%
where the time goes in v1:
time: 838 us; the launch traced here: 826 us
  waiting for transfers between devices  281 us (34%)
  blocking collectives  270 us (32%)
  local copies, waits for them, and re-layouts  143 us (17%)
  other arithmetic  47.2 us (6%)
  starting transfers between devices  37.3 us (4%)
  matrix products  31.9 us (4%)
  between operations  15.6 us (2%)
    ppermute x4, waiting for transfers between devices, from_behind(): return lax.ppermute(block, axis, route)  213 us
    all_gather x5, blocking collectives, local(): lax.all_gather(own_d.astype(jnp.bfloat16), 'tensor', axis=1, tiled=True)  78.7 us
    unnamed x1, blocking collectives  76.2 us
    psum x1, blocking collectives, local(): jax.lax.psum((scale_part, gain_part), axis_name='dp')  71.7 us
    all_gather x1, waiting for transfers between devices, local(): lax.all_gather(master[0].astype(jnp.bfloat16), 'dp', axis=0, tiled=True)  50.7 us
    another operation x23, local copies, waits for them, and re-layouts  32.1 us
    psum x1, blocking collectives, local(): jax.lax.psum(jax.lax.psum((scale_part, gain_part), axis_name='dp'), axis_...  25.9 us
    dynamic_update_slice x15, local copies, waits for them, and re-layouts, store_slot(): return lax.dynamic_update_index_in_dim(buffer, value, slot_index, 0)  21.4 us
  transfers between devices with their start and end apart: 12, of which 8 were waited for; matrix products, arithmetic and copies ran while one was open for 18% of the time, Pallas kernels for 0%

profile of v1, /device:TPU:128, one launch (start us, length us, event | category | flops | bytes accessed | tf_op | source)
XLA Modules:
  0.0 826.4 jit_solution(16303371203682361164)
XLA Ops:
  9.8 17.2 %all-gather = bf16[1,2,1,128,1600]{4,3,2,1,0:T(8,128)(2,1)S(1)} all-gather(bf16[1,2,1,16,1600]{4,3,2,1,0:T(8,128)(2,1)} %param.17), channel_id=2, replica_groups=mesh['pipe'=4,'dp'=16,'tensor'=8] {'tensor'}, dimensions={3}, use_global_device_ids=true | all-gather | bytes 921600 | tf_op jit(solution)/shard_map/all_gather | solution.py:54
  28.1 50.7 %all-gather.9.cloned.1.call-done = bf16[16,100,1024]{2,1,0:T(8,128)(2,1)} async-done(((bf16[1,100,1024]{2,1,0:T(8,128)(2,1)}), bf16[16,100,1024]{2,1,0:T(8,128)(2,1)}) %all-gather.9.cloned.1.call-update) | async-done | bytes 3276816 | tf_op jit(solution)/shard_map/all_gather | solution.py:51
  78.8 2.9 reshape.819
  81.7 3.4 fusion.113
  96.1 2.1 convolution_convert_fusion.20
  98.2 2.3 conditional.5
  100.5 2.0 copy.213
  102.5 4.8 all-to-all-start
  108.7 2.3 constant_dynamic-slice_fusion
  111.4 2.4 copy.217
  115.1 5.5 all-to-all-done
  122.4 15.6 %all-gather.1 = bf16[128,1600]{1,0:T(8,128)(2,1)} all-gather(bf16[16,1600]{1,0:T(8,128)(2,1)S(1)} %convert_element_type.421), channel_id=3, replica_groups=mesh['pipe'=4,'dp'=16,'tensor'=8] {'tensor'}, dimensions={0}, use_global_device_ids=true | all-gather | bytes 460800 | tf_op jit(solution)/shard_map/all_gather | solution.py:139
  138.0 1.9 copy.216
  141.5 2.2 fusion.145
  143.8 2.1 collective-permute-start
  147.2 39.6 %collective-permute-done = bf16[1,128,1600]{1,2,0:T(8,128)(2,1)} collective-permute-done((bf16[1,128,1600]{1,2,0:T(8,128)(2,1)}, bf16[1,128,1600]{1,2,0:T(8,128)(2,1)}, u32[]{:S(2)}, u32[]{:S(2)}) %collective-permute-start) | collective-permute-done | bytes 409632 | tf_op jit(solution)/shard_map/ppermute | solution.py:20
  186.9 1.9 bitcast_dynamic-update-slice_fusion.2
  189.9 2.7 conditional.6
  192.6 2.0 copy.227
  194.6 4.1 all-to-all-start.1
  198.7 2.4 copy.231
  201.1 10.9 %all-to-all-done.1 = bf16[1,8,16,1600]{3,2,0,1:T(8,128)(2,1)} async-done(((bf16[1,8,16,1600]{3,2,0,1:T(8,128)(2,1)}), bf16[1,8,16,1600]{3,2,0,1:T(8,128)(2,1)}, u32[]{:S(2)}, u32[]{:S(2)}) %all-to-all-start.1) | async-done | bytes 409632 | tf_op jit(solution)/shard_map/all_to_all | solution.py:137
  213.7 15.6 %all-gather.2 = bf16[128,1600]{1,0:T(8,128)(2,1)} all-gather(bf16[16,1600]{1,0:T(8,128)(2,1)S(1)} %convert_element_type.429), channel_id=4, replica_groups=mesh['pipe'=4,'dp'=16,'tensor'=8] {'tensor'}, dimensions={0}, use_global_device_ids=true | all-gather | bytes 460800 | tf_op jit(solution)/shard_map/all_gather | solution.py:139
  229.2 2.0 copy.230
  232.9 2.2 fusion.139
  235.1 2.2 collective-permute-start.1
  237.3 98.2 %collective-permute-done.1 = bf16[1,128,1600]{1,2,0:T(8,128)(2,1)} collective-permute-done((bf16[1,128,1600]{1,2,0:T(8,128)(2,1)}, bf16[1,128,1600]{1,2,0:T(8,128)(2,1)}, u32[]{:S(2)}, u32[]{:S(2)}) %collective-permute-start.1) | collective-permute-done | bytes 409632 | tf_op jit(solution)/shard_map/ppermute | solution.py:20
  335.5 2.1 bitcast_dynamic-update-slice_fusion.1
  337.7 34.1 %conditional.7 = (bf16[1,128,1600]{1,2,0:T(8,128)(2,1)}, bf16[1,1,128,768]{3,2,0,1:T(8,128)(2,1)}, bf16[1,1,128,1600]{2,3,0,1:T(8,128)(2,1)}) conditional(s32[]{:T(128)} %convert_element_type.434, () %tuple.72, (s32[]{:T(128)}, bf16[2,1,128,2,128]{4,2,3,0,1:T(8,128)(2,1)}, f32[2,1,2,128,128]{3,4,2,0,1:T(8,128)S(1)}, f32[1,1600]{1,0:T(1,128)S(1)}, ...), branch_computations={%region_11.12_spmd, %region_12.13_spmd} | conditional | flops 454803200 | bytes 11565162 | solution.py:133
  337.7 2.0 copy.236
  369.8 2.0 copy.364
  371.8 2.0 copy.241
  373.8 4.1 all-to-all-start.2
  377.9 2.3 copy.245
  380.3 2.3 copy.259
  382.6 2.4 copy.273
  399.1 16.0 %all-gather.3 = bf16[128,1600]{1,0:T(8,128)(2,1)} all-gather(bf16[16,1600]{1,0:T(8,128)(2,1)S(1)} %convert_element_type.437), channel_id=5, replica_groups=mesh['pipe'=4,'dp'=16,'tensor'=8] {'tensor'}, dimensions={0}, use_global_device_ids=true | all-gather | bytes 460800 | tf_op jit(solution)/shard_map/all_gather | solution.py:139
  415.0 1.9 copy.244
  425.6 38.5 %collective-permute-done.2 = bf16[1,128,1600]{1,2,0:T(8,128)(2,1)S(1)} collective-permute-done((bf16[1,128,1600]{1,2,0:T(8,128)(2,1)S(1)}, bf16[1,128,1600]{1,2,0:T(8,128)(2,1)S(1)}, u32[]{:S(2)}, u32[]{:S(2)}) %collective-permute-start.2) | collective-permute-done | bytes 409632 | tf_op jit(solution)/shard_map/ppermute | solution.py:20
  465.1 34.2 %conditional.8 = (bf16[1,128,1600]{1,2,0:T(8,128)(2,1)}, bf16[1,1,128,768]{3,2,0,1:T(8,128)(2,1)}, bf16[1,1,128,1600]{2,3,0,1:T(8,128)(2,1)}) conditional(s32[]{:T(128)} %convert_element_type.442, () %tuple.74, (s32[]{:T(128)}, bf16[2,1,128,2,128]{4,2,3,0,1:T(8,128)(2,1)}, f32[2,1,2,128,128]{3,4,2,0,1:T(8,128)S(1)}, f32[1,1600]{1,0:T(1,128)S(1)}, ...), branch_computations={%region_15.16_spmd, %region_16.17_spmd} | conditional | flops 454803200 | bytes 11565162 | solution.py:133
  465.2 2.0 copy.250
  467.8 1.9 convolution_convert_fusion.12
  497.4 1.9 copy.368
  499.3 2.0 copy.255
  501.3 4.1 all-to-all-start.3
  505.4 1.9 dynamic-slice_bitcast_fusion.2
  524.3 16.0 %all-gather.4 = bf16[128,1600]{1,0:T(8,128)(2,1)} all-gather(bf16[16,1600]{1,0:T(8,128)(2,1)S(1)} %convert_element_type.445), channel_id=6, replica_groups=mesh['pipe'=4,'dp'=16,'tensor'=8] {'tensor'}, dimensions={0}, use_global_device_ids=true | all-gather | bytes 460800 | tf_op jit(solution)/shard_map/all_gather | solution.py:139
  540.3 1.9 copy.258
  543.9 2.2 fusion.127
  546.1 2.1 collective-permute-start.3
  548.2 1.9 dynamic-slice_bitcast_fusion
  553.3 36.9 %collective-permute-done.3 = bf16[1,128,1600]{1,2,0:T(8,128)(2,1)} collective-permute-done((bf16[1,128,1600]{1,2,0:T(8,128)(2,1)}, bf16[1,128,1600]{1,2,0:T(8,128)(2,1)}, u32[]{:S(2)}, u32[]{:S(2)}) %collective-permute-start.3) | collective-permute-done | bytes 409632 | tf_op jit(solution)/shard_map/ppermute | solution.py:20
  590.2 2.2 bitcast_dynamic-update-slice_fusion.3
  592.4 2.3 conditional.9
  594.7 2.0 copy.269
  596.7 4.1 all-to-all-start.4
  602.5 1.9 bitcast_convert_fusion
  608.2 76.2 %fusion = bf16[112,1024]{1,0:T(8,128)(2,1)} fusion(bf16[1600,1024]{1,0:T(8,128)(2,1)S(1)} %pad_maximum_fusion.5), kind=kCustom, calls=%all-reduce-scatter | all-reduce-scatter fusion | flops 1835009 | bytes 3508224
  685.4 3.7 collective-permute-start.4
  689.1 4.1 collective-permute-start.5
  693.2 2.0 fusion.112
  703.2 15.6 %all-gather.5 = bf16[128,1600]{1,0:T(8,128)(2,1)S(1)} all-gather(bf16[16,1600]{1,0:T(8,128)(2,1)S(1)} %get-tuple-element.432), channel_id=7, replica_groups=mesh['pipe'=4,'dp'=16,'tensor'=8] {'tensor'}, dimensions={0}, use_global_device_ids=true | all-gather | bytes 460800 | tf_op jit(solution)/shard_map/all_gather | solution.py:139
  721.0 71.7 %all-reduce.2 = (f32[1600]{0:T(1024)S(1)}, f32[1600]{0:T(1024)S(1)}) all-reduce(f32[1600]{0:T(1024)S(1)} %select_add_fusion, f32[1600]{0:T(1024)S(1)} %fusion.112), channel_id=1, replica_groups=mesh['pipe'=4,'dp'=16,'tensor'=8] {'dp'}, use_global_device_ids=true, to_apply=%region_32.33 | all-reduce | flops 3200 | bytes 25600 | tf_op jit(solution)/shard_map/psum | solution.py:177
  792.8 25.9 %all-reduce.3 = (f32[1,1600]{1,0:T(1,128)S(1)}, f32[1,1600]{1,0:T(1,128)S(1)}) all-reduce(f32[1,1600]{1,0:T(1,128)S(1)} %stack.10, f32[1,1600]{1,0:T(1,128)S(1)} %stack.9), channel_id=1, replica_groups=mesh['pipe'=4,'dp'=16,'tensor'=8] {'tensor'}, use_global_device_ids=true, to_apply=%region_33.34 | all-reduce | flops 3200 | bytes 25600 | tf_op jit(solution)/shard_map/psum | solution.py:176
  (216 shorter events, 153.9 us)
Async XLA Ops:
  7.2 20.1 %copy-start.2 = (bf16[2,1,128,1600]{2,3,1,0:T(8,128)(2,1)S(1)}, bf16[2,1,128,1600]{2,3,1,0:T(8,128)(2,1)}, u32[]{:S(2)}) copy-start(bf16[2,1,128,1600]{2,3,1,0:T(8,128)(2,1)} %param.18) | copy-start | bytes 2457604
  7.2 71.6 %all-gather.9.cloned.1.call-start = ((), (), s32[]{:S(2)}) async-start(), calls=%async_computation.5 | async-start | bytes 3620864 | tf_op jit(solution)/shard_map/all_gather | solution.py:51
  27.0 1.1 copy-start.5
  27.3 54.4 %copy-start.44 = (f32[2,128]{1,0:T(2,128)}, f32[2,128]{1,0:T(2,128)S(1)}, u32[]{:S(2)}) copy-start(f32[2,128]{1,0:T(2,128)S(1)} %add_rsqrt_fusion) | copy-start | bytes 3076
  81.7 3.5 copy-start.1
  88.3 0.8 copy-start.35
  88.3 5.4 copy-start.34
  93.7 4.5 copy-start.42
  102.5 18.2 %all-to-all-start = ((bf16[1,8,16,1600]{3,2,0,1:T(8,128)(2,1)}), bf16[1,8,16,1600]{3,2,0,1:T(8,128)(2,1)}, u32[]{:S(2)}, u32[]{:S(2)}) async-start(bf16[1,8,16,1600]{3,2,0,1:T(8,128)(2,1)} %bitcast.535), calls=%async_computation | async-start | bytes 851968 | tf_op jit(solution)/shard_map/all_to_all | solution.py:137
  108.6 2.7 copy-start
  121.7 0.6 copy-start.26
  139.9 1.6 copy-start.11
  143.8 43.1 %collective-permute-start = (bf16[1,128,1600]{1,2,0:T(8,128)(2,1)}, bf16[1,128,1600]{1,2,0:T(8,128)(2,1)}, u32[]{:S(2)}, u32[]{:S(2)}) collective-permute-start(bf16[1,128,1600]{1,2,0:T(8,128)(2,1)} %fusion.145), channel_id=1, source_target_pairs={{128,0},{256,128},{384,256},{129,1},{257,129},{385,257},{130,2},{2... | collective-permute-start | bytes 1228808 | tf_op jit(solution)/shard_map/ppermute | solution.py:20
  145.9 41.0 %copy-start.3 = (bf16[2,1,128,1600]{2,3,1,0:T(8,128)(2,1)S(1)}, bf16[2,1,128,1600]{2,3,1,0:T(8,128)(2,1)}, u32[]{:S(2)}) copy-start(bf16[2,1,128,1600]{2,3,1,0:T(8,128)(2,1)} %param.18) | copy-start | bytes 2457604
  188.8 1.1 copy-start.25
  194.6 17.4 %all-to-all-start.1 = ((bf16[1,8,16,1600]{3,2,0,1:T(8,128)(2,1)}), bf16[1,8,16,1600]{3,2,0,1:T(8,128)(2,1)}, u32[]{:S(2)}, u32[]{:S(2)}) async-start(bf16[1,8,16,1600]{3,2,0,1:T(8,128)(2,1)} %bitcast.537), calls=%async_computation.1 | async-start | bytes 851968 | tf_op jit(solution)/shard_map/all_to_all | solution.py:137
  213.0 0.6 copy-start.28
  231.2 1.6 copy-start.9
  235.1 100.4 %collective-permute-start.1 = (bf16[1,128,1600]{1,2,0:T(8,128)(2,1)}, bf16[1,128,1600]{1,2,0:T(8,128)(2,1)}, u32[]{:S(2)}, u32[]{:S(2)}) collective-permute-start(bf16[1,128,1600]{1,2,0:T(8,128)(2,1)} %fusion.139), channel_id=1, source_target_pairs={{128,0},{256,128},{384,256},{129,1},{257,129},{385,257},{130,2},{2... | collective-permute-start | bytes 1228808 | tf_op jit(solution)/shard_map/ppermute | solution.py:20
  364.7 1.6 copy-start.20
  373.8 23.6 %all-to-all-start.2 = ((bf16[1,8,16,1600]{3,2,0,1:T(8,128)(2,1)}), bf16[1,8,16,1600]{3,2,0,1:T(8,128)(2,1)}, u32[]{:S(2)}, u32[]{:S(2)}) async-start(bf16[1,8,16,1600]{3,2,0,1:T(8,128)(2,1)} %bitcast.534), calls=%async_computation.2 | async-start | bytes 851968 | tf_op jit(solution)/shard_map/all_to_all | solution.py:137
  398.4 0.7 copy-start.30
  417.0 1.6 copy-start.8
  417.0 5.1 copy-start.41
  418.6 45.4 %copy-start.4 = (bf16[2,1,128,1600]{2,3,1,0:T(8,128)(2,1)S(1)}, bf16[2,1,128,1600]{2,3,1,0:T(8,128)(2,1)}, u32[]{:S(2)}) copy-start(bf16[2,1,128,1600]{2,3,1,0:T(8,128)(2,1)} %param.18) | copy-start | bytes 2457604
  420.1 45.0 %copy-start.22 = (bf16[1,128,1600]{1,2,0:T(8,128)(2,1)}, bf16[1,128,1600]{1,2,0:T(8,128)(2,1)S(1)}, u32[]{:S(2)}) copy-start(bf16[1,128,1600]{1,2,0:T(8,128)(2,1)S(1)} %fusion.133) | copy-start | bytes 1228804
  420.1 43.9 %collective-permute-start.2 = (bf16[1,128,1600]{1,2,0:T(8,128)(2,1)S(1)}, bf16[1,128,1600]{1,2,0:T(8,128)(2,1)S(1)}, u32[]{:S(2)}, u32[]{:S(2)}) collective-permute-start(bf16[1,128,1600]{1,2,0:T(8,128)(2,1)S(1)} %fusion.133), channel_id=1, source_target_pairs={{128,0},{256,128},{384,256},{129,1},{257,129},{385,257},{130,2},{2... | collective-permute-start | bytes 1228808 | tf_op jit(solution)/shard_map/ppermute | solution.py:20
  422.1 43.0 %copy-start.36 = (bf16[3,1,16,1600]{3,2,0,1:T(8,128)(2,1)}, bf16[3,1,16,1600]{3,2,0,1:T(8,128)(2,1)S(1)}, u32[]{:S(2)}) copy-start(bf16[3,1,16,1600]{3,2,0,1:T(8,128)(2,1)S(1)} %constant_dynamic-update-slice_fusion.14) | copy-start | bytes 460804
  492.2 1.6 copy-start.21
  501.3 21.3 %all-to-all-start.3 = ((bf16[1,8,16,1600]{3,2,0,1:T(8,128)(2,1)}), bf16[1,8,16,1600]{3,2,0,1:T(8,128)(2,1)}, u32[]{:S(2)}, u32[]{:S(2)}) async-start(bf16[1,8,16,1600]{3,2,0,1:T(8,128)(2,1)} %bitcast.536), calls=%async_computation.3 | async-start | bytes 851968 | tf_op jit(solution)/shard_map/all_to_all | solution.py:137
  523.7 0.6 copy-start.32
  542.3 1.6 copy-start.7
  546.1 44.2 %collective-permute-start.3 = (bf16[1,128,1600]{1,2,0:T(8,128)(2,1)}, bf16[1,128,1600]{1,2,0:T(8,128)(2,1)}, u32[]{:S(2)}, u32[]{:S(2)}) collective-permute-start(bf16[1,128,1600]{1,2,0:T(8,128)(2,1)} %fusion.127), channel_id=1, source_target_pairs={{128,0},{256,128},{384,256},{129,1},{257,129},{385,257},{130,2},{2... | collective-permute-start | bytes 1228808 | tf_op jit(solution)/shard_map/ppermute | solution.py:20
  594.7 7.8 copy-start.6
  594.7 7.8 copy-start.45
  596.7 103.9 %all-to-all-start.4 = ((bf16[1,8,16,1600]{3,2,0,1:T(8,128)(2,1)}), bf16[1,8,16,1600]{3,2,0,1:T(8,128)(2,1)}, u32[]{:S(2)}, u32[]{:S(2)}) async-start(bf16[1,8,16,1600]{3,2,0,1:T(8,128)(2,1)} %bitcast.151), calls=%async_computation.4 | async-start | bytes 851968 | tf_op jit(solution)/shard_map/all_to_all | solution.py:137
  602.5 3.8 copy-start.12
  684.4 11.5 %copy-start.24 = (bf16[112,1024]{1,0:T(8,128)(2,1)S(1)}, bf16[112,1024]{1,0:T(8,128)(2,1)}, u32[]{:S(2)}) copy-start(bf16[112,1024]{1,0:T(8,128)(2,1)} %fusion) | copy-start | bytes 688132
  685.4 10.5 %collective-permute-start.4 = (bf16[112,1024]{1,0:T(8,128)(2,1)}, bf16[112,1024]{1,0:T(8,128)(2,1)S(1)}, u32[]{:S(2)}, u32[]{:S(2)}) collective-permute-start(bf16[112,1024]{1,0:T(8,128)(2,1)} %fusion), channel_id=1, source_target_pairs={{0,8},{8,16},{16,24},{24,32},{32,40},{40,48},{48,56},{56,64},{64,7... | collective-permute-start | bytes 688136
  689.1 6.8 collective-permute-start.5
  693.2 3.4 copy-start.23
  693.2 3.4 copy-start.38
  693.2 3.4 copy-start.39
  697.1 4.7 copy-start.27
  697.1 4.7 copy-start.29
  697.1 4.7 copy-start.31
  697.1 4.7 copy-start.33
  700.6 18.5 %copy-start.10 = (f32[1,1,128,1600]{2,3,1,0:T(8,128)S(1)}, f32[1,1,128,1600]{2,3,1,0:T(8,128)}, u32[]{:S(2)}) copy-start(f32[1,1,128,1600]{2,3,1,0:T(8,128)} %copy.273) | copy-start | bytes 2457604
  703.2 16.3 %copy-start.17 = (bf16[1,128,1600]{1,2,0:T(8,128)(2,1)S(1)}, bf16[1,128,1600]{1,2,0:T(8,128)(2,1)}, u32[]{:S(2)}) copy-start(bf16[1,128,1600]{1,2,0:T(8,128)(2,1)} %get-tuple-element.410) | copy-start | bytes 1228804
  703.2 16.3 %copy-start.46 = (f32[16]{0:T(128)S(1)}, f32[16]{0:T(128)}, u32[]{:S(2)}) copy-start(f32[16]{0:T(128)} %dynamic-slice.8) | copy-start | bytes 196
  719.4 0.9 copy-start.37
Sparse Core Ops, SparseCore 0:
  11.6 67.1 all-gather.8
